TPU v7x, 512 devices: a whole 4x8x8 slice. The times are simulated.
512 devices in a mesh: inner: 16 (over z, x_lo), outer: 32 (over y, x_hi, core).
Axes of the slice: x: 4 (x_hi: 2, x_lo: 2; x = x_hi * 2 + x_lo), y: 8, z: 8, core: 2. Of those that a mesh axis runs over, the one named last changes fastest.
Arguments:
- points: bfloat16 [32, 4096, 1024], P('outer', 'inner'), may hold values from -6 to 6
- anchor_index: int32 [32, 2048], P('outer', 'inner'), may hold values from 0 to 255
- norm_gain: float32 [1024], replicated, may hold values from 0.1 to 1.9
- weight_mean: bfloat16 [1024, 1536], P('outer'), may hold values from -0.25 to 0.25
- weight_scale: float32 [1536], replicated, may hold values from 0.01 to 0.04
- noise_seed: int32 [1536], replicated, may hold values from 0 to 16777215
- out_weight: bfloat16 [512, 1024], P('outer'), may hold values from -0.75 to 0.75
- cotangent: bfloat16 [32, 2048, 1024], P('outer', 'inner'), may hold values from -6 to 6
Outputs:
- attended: bfloat16 [32, 2048, 1024], P('outer', 'inner')
- grad_points: float32 [32, 4096, 1024], P('outer', 'inner')
- grad_scale: float32 [1536], replicated
All inputs are finite; a program needn't handle non-finite values.
Results may differ from a plain program's by a relative error of at most 0.022.
The roundings to bfloat16 on the way count: a program that leaves them out, or rounds other values in their place, can miss the bound.
Values may be sent and summed in bfloat16 or wider, within the bound.
A program may use at most 64 MiB of HBM per device.

v0:
```python
import jax
import jax.numpy as jnp
from jax import lax
from jax.sharding import PartitionSpec as P

HEADS = 8


def hashed_noise(seeds, row_count):
    row_ids = jnp.arange(row_count, dtype=jnp.int32)[:, None]
    hashed = seeds[None, :] * 747796405 + row_ids * 1103515245 + 12345
    hashed = hashed ^ hashed >> 15 & 131071
    hashed = hashed * 277803737
    hashed = hashed ^ hashed >> 16 & 65535
    fraction = (hashed >> 8 & 65535).astype(jnp.float32) / 65536.0 + 1.0 / 131072.0
    return (fraction - 0.5) * 3.4641016


def rms_normalize(values, norm_gain):
    mean_square = jnp.mean(values * values, axis=-1, keepdims=True)
    return values * lax.rsqrt(mean_square + 1e-06) * norm_gain


def split_heads(block_rows, value_width, head_count):
    row_count = block_rows.shape[0]
    head_dim = value_width // head_count
    key_h = block_rows[:, :value_width].reshape(row_count, head_count, head_dim)
    value_h = block_rows[:, value_width:].reshape(row_count, head_count, head_dim)
    return (key_h, value_h)


def forward_keys(query_h, block_rows, value_width, score_scale):
    key_h, value_h = split_heads(block_rows, value_width, query_h.shape[1])
    scores = (
        jnp.einsum("qhd,khd->hqk", query_h, key_h, preferred_element_type=jnp.float32) * score_scale
    )
    weights = jnp.exp(scores)
    part_sums = jnp.einsum(
        "hqk,khd->qhd", weights.astype(jnp.bfloat16), value_h, preferred_element_type=jnp.float32
    )
    return (jnp.sum(weights, axis=-1), part_sums)


def local(
    points, anchor_index, norm_gain, weight_mean, weight_scale, noise_seed, out_weight, cotangent
):
    local_points = points[0]
    local_index = anchor_index[0]
    local_cotangent = cotangent[0]
    tok_rows = local_index.shape[0]
    point_rows = local_points.shape[0]
    width = local_points.shape[1]
    selector = (local_index[:, None] == jnp.arange(point_rows, dtype=jnp.int32)[None, :]).astype(
        jnp.bfloat16
    )
    anchors = jnp.dot(selector, local_points, preferred_element_type=jnp.float32).astype(
        jnp.bfloat16
    )
    mean_full, out_full = (
        lax.all_gather(weight_mean, "outer", axis=0, tiled=True),
        lax.all_gather(out_weight, "outer", axis=0, tiled=True),
    )
    noise = hashed_noise(noise_seed, width)
    weight_full = (mean_full.astype(jnp.float32) + weight_scale[None, :] * noise).astype(
        jnp.bfloat16
    )
    value_width = out_full.shape[0]
    head_count = HEADS
    head_dim = value_width // head_count
    score_scale = head_dim ** (-0.5)
    anchors_f = anchors.astype(jnp.float32)
    normed = rms_normalize(anchors_f, norm_gain).astype(jnp.bfloat16)
    projected = jnp.dot(normed, weight_full, preferred_element_type=jnp.float32).astype(
        jnp.bfloat16
    )
    query_h = projected[:, :value_width].reshape(tok_rows, head_count, head_dim)
    key_vals = projected[:, value_width:]
    length = tok_rows * lax.axis_size("inner")
    span = min(512, length)
    zero_totals = jnp.zeros((head_count, tok_rows), jnp.float32)
    zero_sums = jnp.zeros((tok_rows, head_count, head_dim), jnp.float32)
    all_keys = lax.all_gather(key_vals, "inner", axis=0, tiled=True)

    def forward_step(block_index, carried):
        block_rows = lax.dynamic_slice_in_dim(all_keys, block_index * span, span, 0)
        part_totals, part_sums = forward_keys(query_h, block_rows, value_width, score_scale)
        return (carried[0] + part_totals, carried[1] + part_sums)

    totals, summed = lax.fori_loop(0, length // span, forward_step, (zero_totals, zero_sums))
    attention = (summed / totals.T[:, :, None]).astype(jnp.bfloat16).reshape(tok_rows, value_width)
    attended = jnp.dot(attention, out_full, preferred_element_type=jnp.float32).astype(jnp.bfloat16)
    grad_attention = jnp.einsum(
        "td,hd->th", local_cotangent, out_full, preferred_element_type=jnp.float32
    ).astype(jnp.bfloat16)
    grad_h = grad_attention.reshape(tok_rows, head_count, head_dim)
    attention_h = attention.reshape(tok_rows, head_count, head_dim)
    delta_heads = jnp.sum(grad_h.astype(jnp.float32) * attention_h.astype(jnp.float32), axis=-1).T

    def backward_step(block_index, carried):
        grad_query, tables = carried
        first_row = block_index * span
        block_rows = lax.dynamic_slice_in_dim(all_keys, first_row, span, 0)
        key_h, value_h = split_heads(block_rows, value_width, head_count)
        scores = (
            jnp.einsum("qhd,khd->hqk", query_h, key_h, preferred_element_type=jnp.float32)
            * score_scale
        )
        probs = jnp.exp(scores) / totals[:, :, None]
        grad_probs = jnp.einsum("qhd,khd->hqk", grad_h, value_h, preferred_element_type=jnp.float32)
        grad_scores = (probs * (grad_probs - delta_heads[:, :, None])).astype(jnp.bfloat16)
        grad_query = grad_query + jnp.einsum(
            "hqk,khd->qhd", grad_scores, key_h, preferred_element_type=jnp.float32
        )
        probs_all = lax.dynamic_update_slice_in_dim(
            tables[0], probs.astype(jnp.bfloat16), first_row, 2
        )
        scores_all = lax.dynamic_update_slice_in_dim(tables[1], grad_scores, first_row, 2)
        tables = (probs_all, scores_all)
        return (grad_query, tables)

    empty_table = jnp.zeros((head_count, tok_rows, length), jnp.bfloat16)
    start_tables = (empty_table, empty_table)
    grad_query, tables = lax.fori_loop(0, length // span, backward_step, (zero_sums, start_tables))
    grad_query = (grad_query * score_scale).reshape(tok_rows, value_width)
    scores_part = tables[1]
    probs_part = tables[0]
    key_grad = (
        jnp.einsum("hqk,qhd->khd", scores_part, query_h, preferred_element_type=jnp.float32)
        * score_scale
    )
    value_grad = jnp.einsum("hqk,qhd->khd", probs_part, grad_h, preferred_element_type=jnp.float32)
    key_grads = lax.psum_scatter(
        jnp.concatenate(
            [
                key_grad.reshape(lax.axis_size("inner") * tok_rows, value_width),
                value_grad.reshape(lax.axis_size("inner") * tok_rows, value_width),
            ],
            axis=1,
        ).astype(jnp.bfloat16),
        "inner",
        scatter_dimension=0,
        tiled=True,
    ).astype(jnp.float32)
    grad_projected = jnp.concatenate([grad_query, key_grads], axis=1).astype(jnp.bfloat16)
    grad_normed = jnp.einsum(
        "tc,dc->td", grad_projected, weight_full, preferred_element_type=jnp.float32
    )
    weight_grad = jnp.einsum(
        "td,tc->dc", normed, grad_projected, preferred_element_type=jnp.float32
    )
    scale_part = jnp.sum(weight_grad * noise, axis=0)
    grad_scale = lax.psum(scale_part, ("inner", "outer"))
    pullback = jax.vjp(lambda values: rms_normalize(values, norm_gain), anchors_f)[1]
    grad_anchors = pullback(grad_normed)[0]
    grad_local = jnp.einsum(
        "tp,td->pd", selector.astype(jnp.float32), grad_anchors, precision=lax.Precision.HIGHEST
    )
    return (attended[None], grad_local[None], grad_scale)


def solution(mesh):
    in_specs = (
        P("outer", "inner", None),
        P("outer", "inner"),
        P(),
        P("outer", None),
        P(),
        P(),
        P("outer", None),
        P("outer", "inner", None),
    )
    out_specs = (P("outer", "inner", None), P("outer", "inner", None), P())
    return jax.shard_map(local, mesh=mesh, in_specs=in_specs, out_specs=out_specs, check_vma=False)
```

profile of v0, /device:TPU:1, one launch (start us, length us, event | category | flops | bytes accessed | tf_op | source)
XLA Modules:
  0.0 562.4 jit_solution(15191583457407889534)
XLA Ops:
  11.2 94.6 %all-gather.4.cloned.1.call-done = bf16[1024,1536]{1,0:T(8,128)(2,1)} async-done(((bf16[32,1536]{1,0:T(8,128)(2,1)}), bf16[1024,1536]{1,0:T(8,128)(2,1)}) %all-gather.4.cloned.1.call-update) | async-done | bytes 3145744 | tf_op jit(solution)/shard_map/all_gather | solution.py:60
  105.8 5.0 add_convert_fusion
  110.8 1.6 copy-done.1
  114.1 75.2 %all-gather.8.cloned.1.call-done = bf16[512,1024]{1,0:T(8,128)(2,1)} async-done(((bf16[16,1024]{1,0:T(8,128)(2,1)}), bf16[512,1024]{1,0:T(8,128)(2,1)}) %all-gather.8.cloned.1.call-update) | async-done | bytes 1048592 | tf_op jit(solution)/shard_map/all_gather | solution.py:61
  189.3 1.7 convolution_convert_fusion.4
  191.3 98.8 %all-gather.6.cloned.1.call-done = bf16[2048,1024]{1,0:T(8,128)(2,1)} async-done(((bf16[128,1024]{1,0:T(8,128)(2,1)}), bf16[2048,1024]{1,0:T(8,128)(2,1)}) %all-gather.6.cloned.1.call-update) | async-done | bytes 4194320 | tf_op jit(solution)/shard_map/all_gather | solution.py:82
  290.1 6.5 %copy.31 = bf16[2048,1024]{0,1:T(8,128)(2,1)} copy(bf16[2048,1024]{1,0:T(8,128)(2,1)} %all-gather.6.cloned.1.call-done) | data formatting | bytes 8388608
  296.6 9.8 %while.34 = (s32[]{:T(128)}, f32[8,128]{1,0:T(8,128)S(1)}, f32[128,8,64]{0,2,1:T(8,128)S(1)}, bf16[2048,1024]{0,1:T(8,128)(2,1)}, bf16[128,8,64]{0,2,1:T(8,128)(...) while((s32[]{:T(128)}, f32[8,128]{1,0:T(8,128)S(1)}, ...), condition=%wide.region_3.0_spmd.clone, body=%wide.region_1.0_spmd.clone.sunk | while | flops 136446976 | bytes 8011962 | solution.py:89
  299.0 1.3 fusion.53
  301.5 1.3 fusion.53
  303.9 1.3 fusion.53
  306.4 2.5 broadcast_in_dim.36.clone
  308.9 2.5 broadcast_in_dim.36
  311.4 19.3 %while.35 = (s32[]{:T(128)}, f32[128,8,64]{0,2,1:T(8,128)S(1)}, bf16[8,128,2048]{1,2,0:T(8,128)(2,1)}, bf16[8,128,2048]{1,2,0:T(8,128)(2,1)}, bf16[2048,1024]{0,...) while((s32[]{:T(128)}, f32[128,8,64]{0,2,1:T(8,128)S(1)}, ...), condition=%wide.region_6.0_spmd.clone, body=%wide.region_5.0_spmd.clone.sunk | while | flops 204603392 | bytes 12853473 | solution.py:123
  312.7 1.7 bitcast_dynamic-update-slice_fusion.4
  314.4 1.5 bitcast_dynamic-update-slice_fusion.5
  317.6 1.7 bitcast_dynamic-update-slice_fusion.4
  319.2 1.5 bitcast_dynamic-update-slice_fusion.5
  321.1 1.3 fusion.61
  322.4 1.7 bitcast_dynamic-update-slice_fusion.4
  324.0 1.5 bitcast_dynamic-update-slice_fusion.5
  327.2 1.6 bitcast_dynamic-update-slice_fusion.4
  328.8 1.5 bitcast_dynamic-update-slice_fusion.5
  330.7 3.9 multiply_convert_fusion.1
  334.7 1.6 convolution_convert_fusion
  336.2 2.6 pad_maximum_fusion
  338.8 6.4 %copy.39 = bf16[2048,1024]{1,0:T(8,128)(2,1)} copy(bf16[2048,1024]{0,1:T(8,128)(2,1)} %pad_maximum_fusion) | data formatting | bytes 8388608
  347.5 100.5 %reduce-scatter.4.cloned.1.call-done = bf16[128,1024]{1,0:T(8,128)(2,1)} async-done(((bf16[2048,1024]{1,0:T(8,128)(2,1)}), bf16[128,1024]{1,0:T(8,128)(2,1)}) %reduce-scatter.4.cloned.1.call-update) | async-done | bytes 262160
  449.1 3.1 multiply_reduce_fusion.1
  452.2 3.9 multiply_reduce_fusion
  456.2 98.0 %psum.7 = f32[1536]{0:T(1024)} all-reduce(f32[1536]{0:T(1024)S(1)} %multiply_reduce_fusion), channel_id=1, replica_groups=mesh['inner'=16,'outer'=32] {'inner','outer'}, use_global_device_ids=true, to_apply=%region_10.0 | all-reduce | flops 1536 | bytes 12288 | tf_op jit(solution)/shard_map/psum | solution.py:152
  554.2 1.7 convolution_bitcast_fusion.2
  (59 shorter events, 20.2 us)
Async XLA Ops:
  7.2 1.6 copy-start
  7.2 105.3 %copy-start.5 = (f32[1024]{0:T(1024)S(1)}, f32[1024]{0:T(1024)}, u32[]{:S(2)}) copy-start(f32[1024]{0:T(1024)} %param.14) | copy-start | bytes 12292
  7.2 98.6 %all-gather.4.cloned.1.call-start = ((), (), s32[]{:S(2)}) async-start(), calls=%async_computation.1 | async-start | bytes 3244032 | tf_op jit(solution)/shard_map/all_gather | solution.py:60
  7.9 181.4 %all-gather.8.cloned.1.call-start = ((), (), s32[]{:S(2)}) async-start(), calls=%async_computation.3 | async-start | bytes 1081344 | tf_op jit(solution)/shard_map/all_gather | solution.py:61
  8.7 281.4 %all-gather.6.cloned.1.call-start = ((), (), s32[]{:S(2)}) async-start(), calls=%async_computation.2 | async-start | bytes 4456448 | tf_op jit(solution)/shard_map/all_gather | solution.py:82
  11.2 178.2 %copy-start.4 = (bf16[1,128,1024]{2,1,0:T(8,128)(2,1)S(1)}, bf16[1,128,1024]{2,1,0:T(8,128)(2,1)}, u32[]{:S(2)}) copy-start(bf16[1,128,1024]{2,1,0:T(8,128)(2,1)} %param.19) | copy-start | bytes 786436
  110.8 1.6 copy-start.1
  113.8 334.1 %reduce-scatter.4.cloned.1.call-start = ((), (), s32[]{:S(2)}) async-start(), calls=%async_computation.4 | async-start | bytes 4456448
  330.7 3.9 copy-start.2
  345.2 1.2 copy-start.3
  452.2 102.0 %copy-start.6 = (s32[1,128]{1,0:T(1,128)S(1)}, s32[1,128]{1,0:T(1,128)}, u32[]{:S(2)}) copy-start(s32[1,128]{1,0:T(1,128)} %param.13) | copy-start | bytes 1540
Sparse Core Ops, SparseCore 0:
  11.4 94.3 all-gather.3
  109.1 80.1 all-gather.7
  192.0 98.0 all-gather.5
  345.3 102.5 reduce-scatter.3
where the time goes:
time: 563 us; the launch traced here: 562 us
  waiting for transfers between devices  370 us (66%)
  blocking collectives  98 us (17%)
  matrix products  37.2 us (7%)
  local copies, waits for them, and re-layouts  33.1 us (6%)
  between operations  13.9 us (2%)
  other arithmetic  9.12 us (2%)
    unnamed x5, waiting for transfers between devices  102 us
    all_gather x1, waiting for transfers between devices, local(): all_keys = lax.all_gather(key_vals, 'inner', axis=0, tiled=True)  98.8 us
    psum x1, blocking collectives, local(): grad_scale = lax.psum(scale_part, ('inner', 'outer'))  98 us
    all_gather x1, waiting for transfers between devices, local(): lax.all_gather(weight_mean, 'outer', axis=0, tiled=True)  94.6 us
    all_gather x1, waiting for transfers between devices, local(): lax.all_gather(out_weight, 'outer', axis=0, tiled=True)  75.2 us
    unnamed x17, local copies, waits for them, and re-layouts  16.9 us
  transfers between devices with their start and end apart: 4, of which 4 were waited for; matrix products, arithmetic and copies ran while one was open for 2% of the time, Pallas kernels for 0%

commit v1 on v0

v1 whole, which is shorter than its diff:
```python
import functools

import jax
import jax.numpy as jnp
from jax import lax
from jax.experimental import pallas as pl
from jax.experimental.pallas import tpu as pltpu
from jax.sharding import PartitionSpec as P

MESH = pl.DeviceIdType.MESH
BF = jnp.bfloat16
F32 = jnp.float32

HEADS = 8
TOK = 128
PTS = 256
D = 1024
HD = 512
NZ = 8
NY = 8
LOG2E = 1.4426950408889634

KV, Q, O = 0, 1, 2
M_KV, M_Q, M_G, M_ATT, M_DQ, M_DKV = range(6)


def left_half(rows):
    return lax.broadcasted_iota(jnp.int32, (rows, 128), 1) < 64


def swap(x):
    return pltpu.roll(x, 64, 1)


def dot(a, b):
    return jnp.dot(a, b, preferred_element_type=F32)


def dot_nt(a, b):
    return lax.dot_general(a, b, (((1,), (1,)), ((), ())), preferred_element_type=F32)


def body(
    points_ref,
    idx_ref,
    gain_ref,
    mean_ref,
    scale_ref,
    seed_ref,
    outw_ref,
    cot_ref,
    att_out,
    gp_out,
    gs_out,
    pts,
    cot,
    mean_buf,
    out_buf,
    noise_buf,
    nhi,
    nlo,
    wbuf,
    anch,
    normed,
    ubuf,
    kv_send,
    q_send,
    g_send,
    kv_buf,
    kv1_buf,
    q_buf,
    g_buf,
    qz,
    gz,
    qgt,
    wexp,
    oacc,
    inv_buf,
    del_buf,
    dq_acc,
    dkvt,
    dkv_own,
    dkv_x,
    dkv_sib,
    dkv_send,
    att_send,
    dq_send,
    att_buf,
    dq_buf,
    dkv_buf,
    ps_buf,
    loc_sem,
    ring_s,
    ring_r,
    xh_s,
    xh_r,
    sib_s,
    sib_r,
    a2a_s,
    a2a_r,
    skv_s,
    skv_r,
    sdk_s,
    sdk_r,
    ps_s,
    ps_r,
):
    inner = lax.axis_index("inner")
    outer = lax.axis_index("outer")
    z = inner // 2
    xl = inner % 2
    y = outer // 4
    xh = (outer // 2) % 2
    c = outer % 2

    def dev(z_, xl_, y_, xh_, c_):
        return {"inner": z_ * 2 + xl_, "outer": (y_ * 2 + xh_) * 2 + c_}

    def xgroup(k):
        g = (xl * 4 + xh * 2 + c + k) % 8
        return dev(z, g // 4, y, (g // 2) % 2, g % 2)

    def zpeer(k):
        return dev((z + k) % NZ, xl, y, xh, c)

    def ypeer(k):
        return dev(z, xl, (y + k) % NY, xh, c)

    def rcopy(src, dst, ssem, rsem, to):
        return pltpu.make_async_remote_copy(
            src_ref=src,
            dst_ref=dst,
            send_sem=ssem,
            recv_sem=rsem,
            device_id=to,
            device_id_type=MESH,
        )

    sends = []

    def start(copy):
        copy.start()
        sends.append(copy)

    ld_pts = pltpu.make_async_copy(points_ref, pts, loc_sem.at[0])
    ld_cot = pltpu.make_async_copy(cot_ref, cot, loc_sem.at[1])
    ld_pts.start()
    ld_cot.start()

    diag = xl == c
    bar = pltpu.get_barrier_semaphore()

    def hpeer(k):
        return dev((z + k) % NZ, c, y, xh, xl)

    for k in range(1, 8):
        for to in (xgroup(k), zpeer(k), ypeer(k)):
            pl.semaphore_signal(bar, inc=1, device_id=to, device_id_type=MESH)

    @pl.when(jnp.logical_not(diag))
    def _():
        for k in range(1, 8):
            pl.semaphore_signal(bar, inc=1, device_id=hpeer(k), device_id_type=MESH)

    @pl.when(diag)
    def _():
        pl.semaphore_wait(bar, 21)

    @pl.when(jnp.logical_not(diag))
    def _():
        pl.semaphore_wait(bar, 28)

    own = outer

    def block(part, row):
        if part == KV:
            return mean_buf.at[row, :, pl.ds(HD, 2 * HD)]
        if part == Q:
            return mean_buf.at[row, :, pl.ds(0, HD)]
        return out_buf.at[row]

    def shard_of(delta, r, core):
        return ((y + delta) % NY * 2 + (xh + r) % 2) * 2 + core

    sibling = dev(z, xl, y, xh, 1 - c)
    partner = dev(z, xl, y, 1 - xh, c)
    up, down = ypeer(1), ypeer(7)

    def ring_copy(part, direction, dist, r):
        delta = (8 - (dist - 1)) % 8 if direction == 0 else dist - 1
        b = block(part, shard_of(delta, r, c))
        return rcopy(
            b,
            b,
            ring_s.at[part, direction, dist - 1, r],
            ring_r.at[part, direction, dist - 1, r],
            up if direction == 0 else down,
        )

    def ring_arrival(part, direction, dist, r):
        delta = (8 - dist) % 8 if direction == 0 else dist
        b = block(part, shard_of(delta, r, c))
        rcopy(
            b,
            b,
            ring_s.at[part, direction, dist - 1, r],
            ring_r.at[part, direction, dist - 1, r],
            up,
        ).wait_recv()

    def sib_copy(part, delta, r):
        b = block(part, shard_of(delta, r, c))
        return rcopy(b, b, sib_s.at[part, delta, r], sib_r.at[part, delta, r], sibling)

    def stage_own(part):
        b = block(part, own)
        start(rcopy(b, b, xh_s.at[part], xh_r.at[part], partner))
        start(ring_copy(part, 0, 1, 0))
        start(ring_copy(part, 1, 1, 0))
        start(sib_copy(part, 0, 0))

    def stage_partner(part):
        b = block(part, shard_of(0, 1, c))
        rcopy(b, b, xh_s.at[part], xh_r.at[part], partner).wait_recv()
        start(ring_copy(part, 0, 1, 1))
        start(ring_copy(part, 1, 1, 1))
        start(sib_copy(part, 0, 1))

    def stage_ring(part, dist, r):
        for direction in (0, 1):
            if dist == 4 and direction != r:
                continue
            ring_arrival(part, direction, dist, r)
            if dist < 3 or (dist == 3 and direction == r):
                start(ring_copy(part, direction, dist + 1, r))
            delta = (8 - dist) % 8 if direction == 0 else dist
            start(sib_copy(part, delta, r))

    def stage_last(part):
        stage_ring(part, 4, 0)
        stage_ring(part, 4, 1)

    def stage_sibling(part):
        for delta in range(8):
            for r in (0, 1):
                b = block(part, shard_of(delta, r, 1 - c))
                rcopy(
                    b, b, sib_s.at[part, delta, r], sib_r.at[part, delta, r], sibling
                ).wait_recv()

    mean_buf[own] = mean_ref[...]
    out_buf[own] = outw_ref[...]
    stage_own(KV)

    def make_normed():
        ld_pts.wait()
        sel_t = (
            lax.broadcasted_iota(jnp.int32, (PTS, TOK), 0) == idx_ref[...]
        ).astype(F32)
        a = dot(sel_t.T.astype(BF), pts[...])
        anch[...] = a
        r = lax.rsqrt(jnp.mean(a * a, axis=-1, keepdims=True) + 1e-06)
        normed[...] = (a * r * gain_ref[...]).astype(BF)

    def make_noise(chunk):
        def step(t, carry):
            row = pl.multiple_of(chunk * 128 + t * 16, 16)
            for col in range(0, 3 * HD, HD):
                cols = pl.ds(col, HD)
                ids = lax.broadcasted_iota(jnp.int32, (16, HD), 0) + row
                h = seed_ref[:, cols] * 747796405 + 12345 + ids * 1103515245
                h = h ^ lax.shift_right_logical(h, jnp.full_like(h, 15))
                h = h * 277803737
                h = h ^ lax.shift_right_logical(h, jnp.full_like(h, 16))
                h = lax.shift_right_logical(h, jnp.full_like(h, 8)) & 65535
                n = (h.astype(F32) - 32767.5) * (3.4641016 / 65536.0)
                noise_buf[pl.ds(row, 16), cols] = n
                hi = n.astype(BF)
                nhi[pl.ds(row, 16), cols] = hi
                nlo[pl.ds(row, 16), cols] = (n - hi.astype(F32)).astype(BF)
            return carry

        lax.fori_loop(0, 8, step, 0)

    def make_u(third):
        cols = pl.ds(third * HD, HD)
        x = normed[...]
        ubuf[:, cols] = dot(x, nhi[:, cols]) + dot(x, nlo[:, cols])

    def form_weight(col, width):
        cols = pl.ds(col, width)

        def step(s, carry):
            row = pl.multiple_of(s * 32, 32)
            w = mean_buf[s, :, cols].astype(F32) + scale_ref[:, cols] * noise_buf[
                pl.ds(row, 32), cols
            ]
            wbuf[pl.ds(row, 32), cols] = w.astype(BF)
            return carry

        lax.fori_loop(0, 32, step, 0)

    def rnd(x):
        return x.astype(BF).astype(F32)

    m128 = left_half(128)
    m64 = left_half(64)

    def project_kv():
        x = normed[...]
        for t in range(2):
            k2 = rnd(dot(x, wbuf[:, pl.ds(HD + 256 * t, 256)]))
            v2 = rnd(dot(x, wbuf[:, pl.ds(2 * HD + 256 * t, 256)]))
            for u in range(2):
                k = k2[:, u * 128 : u * 128 + 128]
                v = v2[:, u * 128 : u * 128 + 128]
                h = 4 * t + 2 * u
                kv_send[h] = jnp.where(m128, k, swap(v)).astype(BF)
                kv_send[h + 1] = jnp.where(m128, swap(k), v).astype(BF)

    def pack_pair(x, h, ref):
        top, bot = x[:64], x[64:]
        ref[h] = jnp.where(m64, top, swap(bot)).astype(BF)
        ref[h + 1] = jnp.where(m64, swap(top), bot).astype(BF)

    def project_q():
        x = normed[...]
        for t in range(2):
            q2 = rnd(dot(x, wbuf[:, pl.ds(256 * t, 256)]))
            for u in range(2):
                pack_pair(q2[:, u * 128 : u * 128 + 128], 4 * t + 2 * u, q_send)

    def project_g():
        ld_cot.wait()
        x = cot[...]
        for t in range(2):
            w = out_buf[pl.ds(16 * t, 16)].reshape(256, D)
            g2 = rnd(dot_nt(x, w))
            for u in range(2):
                pack_pair(g2[:, u * 128 : u * 128 + 128], 4 * t + 2 * u, g_send)

    late = (4, 3, 5, 2, 6, 1, 7)

    def a2a_one(msg, src_buf, dst_buf, k):
        there = (z + k) % NZ
        return rcopy(
            src_buf.at[there], dst_buf.at[z], a2a_s.at[msg, k], a2a_r.at[msg, k], hpeer(k)
        )

    def a2a_start(msg, src_buf, dst_buf):
        for k in late:
            start(a2a_one(msg, src_buf, dst_buf, k))

        @pl.when(diag)
        def _():
            dst_buf[z] = src_buf[z]

        @pl.when(jnp.logical_not(diag))
        def _():
            a2a_one(msg, src_buf, dst_buf, 0).start()

    def a2a_wait(msg, src_buf, dst_buf, k):
        came = (z + 8 - k) % NZ

        def wait():
            rcopy(
                src_buf.at[came],
                dst_buf.at[came],
                a2a_s.at[msg, k],
                a2a_r.at[msg, k],
                hpeer(k),
            ).wait_recv()

        if k == 0:
            pl.when(jnp.logical_not(diag))(wait)
        else:
            wait()
        return came

    order = (0, 1, 7, 2, 6, 3, 5, 4)

    def a2a_wait_all(msg, src_buf, dst_buf):
        for k in order:
            a2a_wait(msg, src_buf, dst_buf, k)

    def skv_copy(zb, k):
        return rcopy(kv_buf.at[0, zb], kv_buf.at[1, zb], skv_s.at[k], skv_r.at[k], sibling)

    def forward_kv():
        for k in order:
            zb = a2a_wait(M_KV, kv_send, kv_buf.at[0], k)
            start(skv_copy(zb, k))

    def ones_kv(half):
        def step(b, carry):
            kv1_buf[half, b] = jnp.where(m128, 1.0, kv_buf[half, b].astype(F32)).astype(BF)
            return carry

        lax.fori_loop(0, 8, step, 0)

    def unpack_q():
        def step(b, carry):
            p = q_buf[b].astype(F32)
            zero = jnp.zeros_like(p)
            full = jnp.concatenate([jnp.where(m64, p, zero), jnp.where(m64, swap(p), zero)], 0)
            qz[pl.ds(pl.multiple_of(b * 128, 128), 128), :] = full.astype(BF)
            return carry

        lax.fori_loop(0, 8, step, 0)

    def unpack_g():
        def step(b, carry):
            p = g_buf[b].astype(F32)
            zero = jnp.zeros_like(p)
            full = jnp.concatenate([jnp.where(m64, zero, swap(p)), jnp.where(m64, zero, p)], 0)
            rows = pl.ds(pl.multiple_of(b * 128, 128), 128)
            gz[rows, :] = full.astype(BF)
            both = full + qz[rows, :].astype(F32)
            qgt[b] = both.T.astype(BF)
            return carry

        lax.fori_loop(0, 8, step, 0)

    RB = 256

    def forward(half, first):
        def step(i, carry):
            row = pl.multiple_of(i * RB, RB)
            rows = pl.ds(row, RB)
            q = qz[rows, :]
            total = None
            for t in range(2):
                keys = kv_buf[half, pl.ds(4 * t, 4)].reshape(512, 128)
                s = dot_nt(q, keys)
                w = jnp.exp2(s * (0.125 * LOG2E))
                wexp[half, rows, pl.ds(512 * t, 512)] = w
                vals = kv1_buf[half, pl.ds(4 * t, 4)].reshape(512, 128)
                part = dot(w.astype(BF), vals)
                total = part if total is None else total + part
            if first:
                oacc[rows, :] = total
            else:
                oacc[rows, :] += total
            return carry

        lax.fori_loop(0, 1024 // RB, step, 0)

    def finish_forward():
        def step(b, carry):
            rows = pl.ds(pl.multiple_of(b * 128, 128), 128)
            o = oacc[rows, :]
            sw = swap(o)
            att = rnd(jnp.where(m128, 0.0, o / jnp.where(m128, 1.0, sw)))
            tot = jnp.where(m128, o, sw)
            inv_buf[rows, :] = 1.0 / tot
            att_send[b] = jnp.where(m64, swap(att[:64]), att[64:]).astype(BF)
            oacc[rows, :] = att
            return carry

        lax.fori_loop(0, 8, step, 0)

    def make_delta():
        def step(b, carry):
            rows = pl.ds(pl.multiple_of(b * 128, 128), 128)
            d = jnp.sum(oacc[rows, :] * gz[rows, :].astype(F32), axis=-1, keepdims=True)
            del_buf[rows, :] = jnp.broadcast_to(d, (128, 128))
            return carry

        lax.fori_loop(0, 8, step, 0)

    def backward(half, first):
        dkvt[...] = jnp.zeros_like(dkvt)

        def step(i, carry):
            rows = pl.ds(pl.multiple_of(i * RB, RB), RB)
            g = gz[rows, :]
            inv = inv_buf[rows, 0:1]
            delta = del_buf[rows, 0:1]
            qt = jnp.concatenate([qgt[2 * i], qgt[2 * i + 1]], axis=1)
            total = None
            for t in range(2):
                cols = pl.ds(512 * t, 512)
                keys = kv_buf[half, pl.ds(4 * t, 4)].reshape(512, 128)
                dp = dot_nt(g, keys)
                p = wexp[half, rows, cols] * inv
                ds = (p * (dp - delta)).astype(BF)
                pb = p.astype(BF)
                part = dot(ds, keys)
                total = part if total is None else total + part
                dkvt[0:64, cols] += dot(qt[0:64], ds)
                dkvt[64:128, cols] += dot(qt[64:128], pb)
            if first:
                dq_acc[rows, :] = total
            else:
                dq_acc[rows, :] += total
            return carry

        lax.fori_loop(0, 1024 // RB, step, 0)

    def key_grads(b):
        x = dkvt[:, pl.ds(b * 128, 128)].T
        return x * jnp.where(m128, 0.125, 1.0)

    def sdk_copy(b):
        return rcopy(dkv_x.at[b], dkv_sib.at[b], sdk_s.at[b], sdk_r.at[b], sibling)

    make_normed()
    stage_partner(KV)
    make_noise(0)
    stage_ring(KV, 1, 0)
    make_noise(1)
    stage_ring(KV, 1, 1)
    make_noise(2)
    stage_ring(KV, 2, 0)
    make_noise(3)
    stage_ring(KV, 2, 1)
    stage_own(Q)
    make_noise(4)
    stage_ring(KV, 3, 0)
    stage_partner(Q)
    make_noise(5)
    stage_ring(KV, 3, 1)
    make_noise(6)
    stage_last(KV)
    make_noise(7)
    stage_ring(Q, 1, 0)
    stage_ring(Q, 1, 1)
    stage_sibling(KV)
    form_weight(HD, 2 * HD)
    stage_ring(Q, 2, 0)
    stage_ring(Q, 2, 1)
    stage_own(O)
    project_kv()
    a2a_start(M_KV, kv_send, kv_buf.at[0])
    stage_ring(Q, 3, 0)
    stage_ring(Q, 3, 1)
    stage_partner(O)
    make_u(0)
    stage_last(Q)
    stage_ring(O, 1, 0)
    stage_ring(O, 1, 1)
    stage_sibling(Q)
    form_weight(0, HD)
    project_q()
    a2a_start(M_Q, q_send, q_buf)
    stage_ring(O, 2, 0)
    stage_ring(O, 2, 1)
    forward_kv()
    stage_ring(O, 3, 0)
    stage_ring(O, 3, 1)
    make_u(1)
    ones_kv(0)
    stage_last(O)
    a2a_wait_all(M_Q, q_send, q_buf)
    unpack_q()
    stage_sibling(O)
    project_g()
    a2a_start(M_G, g_send, g_buf)
    forward(0, True)
    for k in order:
        skv_copy((z + 8 - k) % NZ, k).wait_recv()
    ones_kv(1)
    forward(1, False)
    finish_forward()
    a2a_start(M_ATT, att_send, att_buf)
    a2a_wait_all(M_G, g_send, g_buf)
    unpack_g()
    make_delta()
    backward(1, True)
    for b in range(8):
        dkv_x[b] = key_grads(b).astype(BF)
        start(sdk_copy(b))
    backward(0, False)

    def pack_dq(b, carry):
        x = dq_acc[pl.ds(pl.multiple_of(b * 128, 128), 128), :] * 0.125
        dq_send[b] = jnp.where(m64, x[:64], swap(x[64:])).astype(BF)
        return carry

    lax.fori_loop(0, 8, pack_dq, 0)
    a2a_start(M_DQ, dq_send, dq_buf)
    for b in range(8):
        sdk_copy(b).wait_recv()
        dkv_send[b] = (key_grads(b) + dkv_sib[b].astype(F32)).astype(BF)
    a2a_start(M_DKV, dkv_send, dkv_buf)
    make_u(2)

    def join_pair(a, b):
        a, b = a.astype(F32), b.astype(F32)
        return jnp.concatenate([jnp.where(m64, a, swap(b)), jnp.where(m64, swap(a), b)], 0)

    a2a_wait_all(M_ATT, att_send, att_buf)
    att_all = jnp.concatenate(
        [join_pair(att_buf[h], att_buf[h + 1]).astype(BF) for h in range(0, 8, 2)], axis=1
    )
    for t in range(2):
        w = out_buf[:, :, pl.ds(512 * t, 512)].reshape(HD, 512)
        att_out[:, pl.ds(512 * t, 512)] = dot(att_all, w).astype(BF)

    a2a_wait_all(M_DQ, dq_send, dq_buf)
    grads = [join_pair(dq_buf[h], dq_buf[h + 1]) for h in range(0, 8, 2)]
    a2a_wait_all(M_DKV, dkv_send, dkv_buf)
    dks, dvs = [], []
    for h in range(0, 8, 2):
        a, b = dkv_buf[h].astype(F32), dkv_buf[h + 1].astype(F32)
        dks.append(jnp.where(m128, a, swap(b)))
        dvs.append(jnp.where(m128, swap(a), b))
    gproj = jnp.concatenate(grads + dks + dvs, axis=1)

    ps_buf[0, 0] = jnp.sum(gproj * ubuf[...], axis=0, keepdims=True)
    gproj = gproj.astype(BF)

    def ps_copy(stage, k):
        to = (zpeer, ypeer, xgroup)[stage](k)
        return rcopy(
            ps_buf.at[stage, 0], ps_buf.at[stage, k], ps_s.at[stage, k], ps_r.at[stage, k], to
        )

    def ps_start(stage):
        for k in late:
            start(ps_copy(stage, k))

    def ps_sum(stage):
        for k in order[1:]:
            ps_copy(stage, k).wait_recv()
        place = (z, y, xl * 4 + xh * 2 + c)[stage]
        total = None
        for j in range(8):
            v = ps_buf[stage, (place + 8 - j) % 8]
            total = v if total is None else total + v
        return total

    ps_start(0)
    grad = [dot_nt(gproj, wbuf[pl.ds(512 * t, 512), :]) for t in range(2)]
    grad = jnp.concatenate(grad, axis=1)
    ps_buf[1, 0] = ps_sum(0)
    ps_start(1)
    a = anch[...]
    r = lax.rsqrt(jnp.mean(a * a, axis=-1, keepdims=True) + 1e-06)
    d = grad * gain_ref[...]
    ga = r * (d - a * (r * r * jnp.mean(d * a, axis=-1, keepdims=True)))
    hi = ga.astype(BF)
    lo = (ga - hi.astype(F32)).astype(BF)
    ps_buf[2, 0] = ps_sum(1)
    ps_start(2)
    sel_t = (lax.broadcasted_iota(jnp.int32, (PTS, TOK), 0) == idx_ref[...]).astype(BF)
    sel2 = jnp.concatenate([sel_t, sel_t], axis=1)
    for t in range(2):
        cols = slice(512 * t, 512 * t + 512)
        gp_out[:, cols] = dot(sel2, jnp.concatenate([hi[:, cols], lo[:, cols]], axis=0))
    gs_out[...] = ps_sum(2)

    for copy in sends:
        copy.wait_send()

    @pl.when(jnp.logical_not(diag))
    def _():
        for msg, src, dst in (
            (M_KV, kv_send, kv_buf.at[0]),
            (M_Q, q_send, q_buf),
            (M_G, g_send, g_buf),
            (M_ATT, att_send, att_buf),
            (M_DQ, dq_send, dq_buf),
            (M_DKV, dkv_send, dkv_buf),
        ):
            a2a_one(msg, src, dst, 0).wait_send()


def local(points, anchor_index, norm_gain, weight_mean, weight_scale, noise_seed, out_weight, cotangent):
    vm = pl.BlockSpec(memory_space=pltpu.VMEM)
    hbm = pl.BlockSpec(memory_space=pl.ANY)
    V = pltpu.VMEM
    dma = pltpu.SemaphoreType.DMA
    att, gpts, gs = pl.pallas_call(
        body,
        out_shape=(
            jax.ShapeDtypeStruct((TOK, D), BF),
            jax.ShapeDtypeStruct((PTS, D), F32),
            jax.ShapeDtypeStruct((1, 3 * HD), F32),
        ),
        in_specs=[hbm, vm, vm, vm, vm, vm, vm, hbm],
        out_specs=(vm, vm, vm),
        scratch_shapes=[
            V((PTS, D), BF),
            V((TOK, D), BF),
            V((32, 32, 3 * HD), BF),
            V((32, 16, D), BF),
            V((D, 3 * HD), F32),
            V((D, 3 * HD), BF),
            V((D, 3 * HD), BF),
            V((D, 3 * HD), BF),
            V((TOK, D), F32),
            V((TOK, D), BF),
            V((TOK, 3 * HD), F32),
            V((8, 128, 128), BF),
            V((8, 64, 128), BF),
            V((8, 64, 128), BF),
            V((2, 8, 128, 128), BF),
            V((2, 8, 128, 128), BF),
            V((8, 64, 128), BF),
            V((8, 64, 128), BF),
            V((1024, 128), BF),
            V((1024, 128), BF),
            V((8, 128, 128), BF),
            V((2, 1024, 1024), F32),
            V((1024, 128), F32),
            V((1024, 128), F32),
            V((1024, 128), F32),
            V((1024, 128), F32),
            V((128, 1024), F32),
            V((8, 128), F32),
            V((8, 128, 128), BF),
            V((8, 128, 128), BF),
            V((8, 128, 128), BF),
            V((8, 64, 128), BF),
            V((8, 64, 128), BF),
            V((8, 64, 128), BF),
            V((8, 64, 128), BF),
            V((8, 128, 128), BF),
            V((3, 8, 1, 3 * HD), F32),
            dma((2,)),
            dma((3, 2, 4, 2)),
            dma((3, 2, 4, 2)),
            dma((3,)),
            dma((3,)),
            dma((3, 8, 2)),
            dma((3, 8, 2)),
            dma((6, 8)),
            dma((6, 8)),
            dma((8,)),
            dma((8,)),
            dma((8,)),
            dma((8,)),
            dma((3, 8)),
            dma((3, 8)),
        ],
        compiler_params=pltpu.CompilerParams(
            collective_id=0, has_side_effects=True, vmem_limit_bytes=56 * 1024 * 1024
        ),
    )(
        points[0],
        anchor_index,
        norm_gain.reshape(1, D),
        weight_mean,
        weight_scale.reshape(1, 3 * HD),
        noise_seed.reshape(1, 3 * HD),
        out_weight,
        cotangent[0],
    )
    return att[None], gpts[None], gs.reshape(3 * HD)


def solution(mesh):
    in_specs = (
        P("outer", "inner", None),
        P("outer", "inner"),
        P(),
        P("outer", None),
        P(),
        P(),
        P("outer", None),
        P("outer", "inner", None),
    )
    out_specs = (P("outer", "inner", None), P("outer", "inner", None), P())
    return jax.shard_map(local, mesh=mesh, in_specs=in_specs, out_specs=out_specs, check_vma=False)
```

time: 563 us -> 113 us (0.20)
  waiting for transfers between devices: 370 us -> 0 us
  Pallas kernels: 0 us -> 105 us
  blocking collectives: 98 us -> 0 us
  matrix products: 37.2 us -> 0 us
  local copies, waits for them, and re-layouts: 33.1 us -> 6.56 us
  between operations: 13.9 us -> 0.66 us
  other arithmetic: 9.12 us -> 0.62 us
    all_gather x3 -> x0, waiting for transfers between devices: 269 us -> none  [the longest x1 98.8 us: local(): all_keys = lax.all_gather(key_vals, 'inner', axis=0, tiled=True)]
    pallas_call x0 -> x1, Pallas kernels: none -> 105 us  [local(): pl.pallas_call(body, out_shape=(jax.ShapeDtypeStruct((TOK, D), BF), jax.S...]
    unnamed x5 -> x0, waiting for transfers between devices: 102 us -> none
    psum x1 -> x0, blocking collectives: 98 us -> none  [local(): grad_scale = lax.psum(scale_part, ('inner', 'outer'))]
    dot_general x29 -> x0, matrix products: 37.2 us -> none  [the longest x4 6.61 us: backward_step(): jnp.einsum('qhd,khd->hqk', query_h, key_h, preferred_element_type=jnp.flo...]
    unnamed x17 -> x6, local copies, waits for them, and re-layouts: 16.9 us -> 4.66 us
    slice x11 -> x0, local copies, waits for them, and re-layouts: 11.1 us -> none  [the longest x8 10.2 us: split_heads(): block_rows[:, value_width:].reshape(row_count, head_count, head_dim)]
  transfers between devices with their start and end apart: 4 -> 0, of which waited for: 4 -> 0; matrix products, arithmetic and copies ran while one was open for 2% -> 0% of each run, Pallas kernels for 0% -> 0%
where the time goes in v1:
time: 113 us
  Pallas kernels  105 us (93%)
  local copies, waits for them, and re-layouts  6.56 us (6%)
    pallas_call x1, Pallas kernels, local(): pl.pallas_call(body, out_shape=(jax.ShapeDtypeStruct((TOK, D), BF), jax.S...  105 us
    unnamed x6, local copies, waits for them, and re-layouts  4.66 us

profile of v1, /device:TPU:1, one launch (start us, length us, event | category | flops | bytes accessed | tf_op | source)
XLA Modules:
  0.0 112.7 jit_solution(12496860433641853341)
XLA Ops:
  0.6 0.0 copy-start
  0.6 1.3 %reshape.19.scale_ref = f32[1,1536]{1,0:T(1,128)} reshape(f32[1536]{0:T(1024)} %param.12) | data formatting | bytes 12288 | tf_op jit(solution)/shard_map/reshape | solution.py:745
  1.9 0.0 copy-done
  1.9 0.6 reshape.20.seed_ref
  2.5 104.8 %shard_map.103 = (bf16[128,1024]{1,0:T(8,128)(2,1)}, f32[256,1024]{1,0:T(8,128)}, f32[1,1536]{1,0:T(1,128)}) custom-call(bf16[256,1024]{1,0:T(8,128)(2,1)} %bitcast.6, s32[1,128]{1,0:T(1,128)} %idx_ref.1, f32[1,1024]{1,0:T(1,128)} %bitcast.9, bf16[32,1536]{1,0:T(8,128)(2,1)} %mean_ref.1, f32[1,1536]{1,0:T(1,128)} %reshape.19.scale_ref, ...), custom_call_target="tpu_custom_call" | custom-call | tf_op jit(solution)/shard_map/pallas_call | solution.py:674
  107.4 0.0 copy-start.1
  107.4 0.7 copy-done.1
  108.1 0.6 reduce
  108.7 1.7 %copy.13 = bf16[1,128,1024]{2,1,0:T(8,128)(2,1)} copy(bf16[1,128,1024]{2,1,0:T(8,128)(2,1)} %bitcast.8) | data formatting | bytes 524288
  110.4 2.3 %copy.14 = f32[1,256,1024]{2,1,0:T(8,128)} copy(f32[1,256,1024]{2,1,0:T(8,128)} %bitcast.5) | data formatting | bytes 2097152
Async XLA Ops:
  0.6 1.3 %copy-start = (s32[1536]{0:T(1024)S(1)}, s32[1536]{0:T(1024)}, u32[]{:S(2)}) copy-start(s32[1536]{0:T(1024)} %param.13) | copy-start | bytes 18436
  107.4 0.7 copy-start.1

commit v2 on v1

v2 whole, which is shorter than its diff:
```python
import functools

import jax
import jax.numpy as jnp
from jax import lax
from jax.experimental import pallas as pl
from jax.experimental.pallas import tpu as pltpu
from jax.sharding import PartitionSpec as P

MESH = pl.DeviceIdType.MESH
BF = jnp.bfloat16
F32 = jnp.float32

HEADS = 8
TOK = 128
PTS = 256
D = 1024
HD = 512
NZ = 8
NY = 8
LOG2E = 1.4426950408889634

K, V, Q, O = 0, 1, 2, 3
M_KV, M_Q, M_G, M_UKV, M_UQ, M_ATT, M_DQ, M_DKV = range(8)
AWAY = (4, 3, 5, 0, 2, 6, 1, 7)


def left_half(rows):
    return lax.broadcasted_iota(jnp.int32, (rows, 128), 1) < 64


def swap(x):
    return pltpu.roll(x, 64, 1)


def dot(a, b):
    return jnp.dot(a, b, preferred_element_type=F32)


def dot_nt(a, b):
    return lax.dot_general(a, b, (((1,), (1,)), ((), ())), preferred_element_type=F32)


def body(
    points_hbm,
    idx_hbm,
    gain_hbm,
    mean_hbm,
    scale_hbm,
    seed_hbm,
    outw_hbm,
    cot_hbm,
    att_out,
    hi_out,
    lo_out,
    gs_out,
    idx_out,
    pts,
    cot,
    idx_ref,
    gain_ref,
    mean_ref,
    scale_ref,
    seed_ref,
    outw_ref,
    pbuf,
    obuf,
    ow,
    noise_buf,
    nhi,
    wbuf,
    anch,
    normed,
    kproj,
    kv_send,
    q_send,
    g_send,
    ukv_send,
    uq_send,
    kv_buf,
    kv1_buf,
    q_buf,
    g_buf,
    ukv_buf,
    uq_buf,
    qz,
    gz,
    qgt,
    wexp,
    oacc,
    inv_buf,
    del_buf,
    dq_acc,
    dkvt,
    dkv_x,
    dkv_sib,
    dkv_send,
    att_send,
    dq_send,
    att_buf,
    dq_buf,
    dkv_buf,
    ps_buf,
    loc_sem,
    far_s,
    far_r,
    xo_s,
    xo_r,
    near_s,
    near_r,
    sib_s,
    sib_r,
    a2a_s,
    a2a_r,
    skv_s,
    skv_r,
    sdk_s,
    sdk_r,
    ps_s,
    ps_r,
):
    inner = lax.axis_index("inner")
    outer = lax.axis_index("outer")
    z = inner // 2
    xl = inner % 2
    y = outer // 4
    xh = (outer // 2) % 2
    c = outer % 2

    def dev(z_, xl_, y_, xh_, c_):
        return {"inner": z_ * 2 + xl_, "outer": (y_ * 2 + xh_) * 2 + c_}

    def xgroup(k):
        g = (xl * 4 + xh * 2 + c + k) % 8
        return dev(z, g // 4, y, (g // 2) % 2, g % 2)

    def zpeer(k):
        return dev((z + k) % NZ, xl, y, xh, c)

    def ypeer(k):
        return dev(z, xl, (y + k) % NY, xh, c)

    def rcopy(src, dst, ssem, rsem, to):
        return pltpu.make_async_remote_copy(
            src_ref=src,
            dst_ref=dst,
            send_sem=ssem,
            recv_sem=rsem,
            device_id=to,
            device_id_type=MESH,
        )

    sends = []

    def start(copy):
        copy.start()
        sends.append(copy)

    loads = [
        pltpu.make_async_copy(a, b, loc_sem.at[n])
        for n, (a, b) in enumerate(
            (
                (mean_hbm, mean_ref),
                (outw_hbm, outw_ref),
                (points_hbm, pts),
                (idx_hbm, idx_ref),
                (gain_hbm, gain_ref),
                (seed_hbm, seed_ref),
                (scale_hbm, scale_ref),
                (cot_hbm, cot),
            )
        )
    ]
    for load in loads:
        load.start()

    diag = xl == c
    bar = pltpu.get_barrier_semaphore()

    def hpeer(k):
        return dev((z + k) % NZ, c, y, xh, xl)

    for k in range(1, 8):
        for to in (ypeer(k), xgroup(k), hpeer(k)):
            pl.semaphore_signal(bar, inc=1, device_id=to, device_id_type=MESH)

    @pl.when(jnp.logical_not(diag))
    def _():
        for k in (1, 7):
            pl.semaphore_signal(bar, inc=1, device_id=zpeer(k), device_id_type=MESH)

    colour = (z + 2 * ((xl + xh) % 2)) % 4
    sibling = dev(z, xl, y, xh, 1 - c)
    across = dev(z, 1 - xl, y, 1 - xh, c)
    near = (zpeer(1), zpeer(7), dev(z, 1 - xl, y, xh, c))
    near_add = (3, 1, 2)

    def piece(part, k, core):
        if part == O:
            return obuf.at[k, core]
        return pbuf.at[part, k, core]

    def own_piece():
        loads[0].wait()
        loads[1].wait()
        for part, base in ((K, HD), (V, 2 * HD), (Q, 0)):
            cols = pl.ds(pl.multiple_of(base + colour * 128, 128), 128)
            pbuf[part, colour, c, xh, y] = mean_ref[:, cols]
        cols = pl.ds(pl.multiple_of(colour * 256, 128), 256)
        obuf[colour, c, xh, y] = outw_ref[:, cols]

    def far_copy(part, k, at):
        b = piece(part, colour, c).at[xh, at]
        return rcopy(b, b, far_s.at[part, k], far_r.at[part, k], ypeer(k))

    def gather_far(part):
        for k in (4, 3, 5, 2, 6, 1, 7):
            start(far_copy(part, k, y))

    def half_out(part, r):
        b = piece(part, colour, c).at[(xh + r) % 2]
        for n, to in enumerate(near):
            start(rcopy(b, b, near_s.at[part, r, n], near_r.at[part, r, n], to))
        start(rcopy(b, b, sib_s.at[part, r], sib_r.at[part, r], sibling))

    def gather_mid(part):
        for k in (1, 7, 2, 6, 3, 5, 4):
            far_copy(part, k, (y + 8 - k) % NY).wait_recv()
        b = piece(part, colour, c).at[xh]
        start(rcopy(b, b, xo_s.at[part], xo_r.at[part], across))
        half_out(part, 0)

    def gather_near(part):
        b = piece(part, colour, c).at[1 - xh]
        rcopy(b, b, xo_s.at[part], xo_r.at[part], across).wait_recv()
        half_out(part, 1)

    def sib_copy(part, n, core):
        b = piece(part, (colour + near_add[n]) % 4, core)
        return rcopy(b, b, sib_s.at[part, 2 + n], sib_r.at[part, 2 + n], sibling)

    def gather_sibling(part):
        for n in range(3):
            for r in range(2):
                b = piece(part, (colour + near_add[n]) % 4, c).at[(xh + r) % 2]
                rcopy(b, b, near_s.at[part, r, n], near_r.at[part, r, n], near[n]).wait_recv()
            start(sib_copy(part, n, c))

    def gather_last(part):
        for r in range(2):
            b = piece(part, colour, 1 - c).at[(xh + r) % 2]
            rcopy(b, b, sib_s.at[part, r], sib_r.at[part, r], sibling).wait_recv()
        for n in range(3):
            sib_copy(part, n, 1 - c).wait_recv()

    def make_normed():
        for load in loads[2:5]:
            load.wait()
        sel_t = (
            lax.broadcasted_iota(jnp.int32, (PTS, TOK), 0) == idx_ref[...]
        ).astype(F32)
        a = dot(sel_t.T.astype(BF), pts[...])
        anch[...] = a
        r = lax.rsqrt(jnp.mean(a * a, axis=-1, keepdims=True) + 1e-06)
        normed[...] = (a * r * gain_ref[...]).astype(BF)

    def row_of(ref, col):
        r0 = col // 128
        return jnp.concatenate([ref[r : r + 1, :] for r in range(r0, r0 + 4)], axis=1)

    def make_noise(chunk):
        def step(t, carry):
            row = pl.multiple_of(chunk * 128 + t * 16, 16)
            for col in range(0, 3 * HD, HD):
                cols = pl.ds(col, HD)
                ids = lax.broadcasted_iota(jnp.int32, (16, HD), 0) + row
                h = row_of(seed_ref, col) * 747796405 + 12345 + ids * 1103515245
                h = h ^ lax.shift_right_logical(h, jnp.full_like(h, 15))
                h = h * 277803737
                h = h ^ lax.shift_right_logical(h, jnp.full_like(h, 16))
                h = lax.shift_right_logical(h, jnp.full_like(h, 8)) & 65535
                n = (h.astype(F32) - 32767.5) * (3.4641016 / 65536.0)
                noise_buf[pl.ds(row, 16), cols] = n
                nhi[pl.ds(row, 16), cols] = n.astype(BF)
            return carry

        lax.fori_loop(0, 8, step, 0)

    def rnd(x):
        return x.astype(BF).astype(F32)

    m128 = left_half(128)
    m64 = left_half(64)

    def form_weight(part):
        col = {K: HD, V: 2 * HD, Q: 0}[part]

        def step(s_, carry):
            scale = row_of(scale_ref, col)
            for half, core in ((0, 0), (0, 1), (1, 0), (1, 1)):
                row = pl.multiple_of(s_ * 128 + half * 64 + core * 32, 32)
                for k in range(4):
                    cols = pl.ds(col + 128 * k, 128)
                    w = pbuf[part, k, core, half, s_].astype(F32) + scale[:, 128 * k : 128 * k + 128] * noise_buf[pl.ds(row, 32), cols]
                    wbuf[pl.ds(row, 32), cols] = w.astype(BF)
            return carry

        lax.fori_loop(0, 8, step, 0)

    def form_out():
        def step(s_, carry):
            for half, core in ((0, 0), (0, 1), (1, 0), (1, 1)):
                row = pl.multiple_of(s_ * 64 + half * 32 + core * 16, 16)
                for k in range(4):
                    ow[pl.ds(row, 16), pl.ds(256 * k, 256)] = obuf[k, core, half, s_]
            return carry

        lax.fori_loop(0, 8, step, 0)

    def pack_kv(k2, v2, h0, ref):
        for u in range(2):
            k = k2[:, u * 128 : u * 128 + 128]
            v = v2[:, u * 128 : u * 128 + 128]
            h = h0 + 2 * u
            ref[h] = jnp.where(m128, k, swap(v)).astype(BF)
            ref[h + 1] = jnp.where(m128, swap(k), v).astype(BF)

    def project_k():
        x = normed[...]
        for t in range(2):
            kproj[:, pl.ds(256 * t, 256)] = rnd(dot(x, wbuf[:, pl.ds(HD + 256 * t, 256)]))

    def project_v():
        x = normed[...]
        for t in range(2):
            v2 = rnd(dot(x, wbuf[:, pl.ds(2 * HD + 256 * t, 256)]))
            pack_kv(kproj[:, pl.ds(256 * t, 256)], v2, 4 * t, kv_send)

    def pack_pair(x, h, ref):
        top, bot = x[:64], x[64:]
        ref[h] = jnp.where(m64, top, swap(bot)).astype(BF)
        ref[h + 1] = jnp.where(m64, swap(top), bot).astype(BF)

    def pack_quad(x, t, ref):
        for u in range(2):
            pack_pair(x[:, u * 128 : u * 128 + 128], 4 * t + 2 * u, ref)

    def project_q():
        x = normed[...]
        for t in range(2):
            pack_quad(rnd(dot(x, wbuf[:, pl.ds(256 * t, 256)])), t, q_send)

    def make_ukv():
        x = normed[...]
        for t in range(2):
            k2 = dot(x, nhi[:, pl.ds(HD + 256 * t, 256)])
            v2 = dot(x, nhi[:, pl.ds(2 * HD + 256 * t, 256)])
            pack_kv(k2, v2, 4 * t, ukv_send)

    def make_uq():
        x = normed[...]
        for t in range(2):
            pack_quad(dot(x, nhi[:, pl.ds(256 * t, 256)]), t, uq_send)

    def project_g():
        loads[7].wait()
        x = cot[...]
        for t in range(2):
            pack_quad(rnd(dot_nt(x, ow[pl.ds(256 * t, 256), :])), t, g_send)

    def a2a_one(msg, src_buf, dst_buf, p, back):
        k = AWAY[p]
        if back:
            src, dst, to = src_buf.at[p], dst_buf.at[z], hpeer(8 - k)
        else:
            src, dst, to = src_buf.at[(z + k) % NZ], dst_buf.at[p], hpeer(k)
        return rcopy(src, dst, a2a_s.at[msg, p], a2a_r.at[msg, p], to)

    def a2a_start(msg, src_buf, dst_buf, back=False, slots=range(8)):
        for p in slots:
            if AWAY[p]:
                start(a2a_one(msg, src_buf, dst_buf, p, back))
                continue

            @pl.when(diag)
            def _():
                if back:
                    dst_buf[z] = src_buf[p]
                else:
                    dst_buf[p] = src_buf[z]

            @pl.when(jnp.logical_not(diag))
            def _():
                a2a_one(msg, src_buf, dst_buf, p, back).start()

    def a2a_wait(msg, src_buf, dst_buf, p, back=False):
        k = AWAY[p]

        def wait():
            dst = dst_buf.at[(z + k) % NZ] if back else dst_buf.at[p]
            src = src_buf.at[0]
            rcopy(src, dst, a2a_s.at[msg, p], a2a_r.at[msg, p], hpeer(k)).wait_recv()

        if k == 0:
            pl.when(jnp.logical_not(diag))(wait)
        else:
            wait()

    order = (3, 6, 7, 4, 5, 1, 2, 0)

    def a2a_wait_all(msg, src_buf, dst_buf, back=False):
        for p in order:
            a2a_wait(msg, src_buf, dst_buf, p, back)

    def skv_copy(p):
        return rcopy(kv_buf.at[0, p], kv_buf.at[1, p], skv_s.at[p], skv_r.at[p], sibling)

    def forward_kv():
        for p in order:
            a2a_wait(M_KV, kv_send, kv_buf.at[0], p)
            start(skv_copy(p))

    def ones_kv(half):
        def step(b, carry):
            kv1_buf[half, b] = jnp.where(m128, 1.0, kv_buf[half, b].astype(F32)).astype(BF)
            return carry

        lax.fori_loop(0, 8, step, 0)

    def unpack_q():
        def step(b, carry):
            p = q_buf[b].astype(F32)
            zero = jnp.zeros_like(p)
            full = jnp.concatenate([jnp.where(m64, p, zero), jnp.where(m64, swap(p), zero)], 0)
            qz[pl.ds(pl.multiple_of(b * 128, 128), 128), :] = full.astype(BF)
            return carry

        lax.fori_loop(0, 8, step, 0)

    def unpack_g():
        def step(b, carry):
            p = g_buf[b].astype(F32)
            zero = jnp.zeros_like(p)
            full = jnp.concatenate([jnp.where(m64, zero, swap(p)), jnp.where(m64, zero, p)], 0)
            rows = pl.ds(pl.multiple_of(b * 128, 128), 128)
            gz[rows, :] = full.astype(BF)
            both = full + qz[rows, :].astype(F32)
            qgt[b] = both.T.astype(BF)
            return carry

        lax.fori_loop(0, 8, step, 0)

    RB = 256

    def forward(half, first):
        def step(i, carry):
            row = pl.multiple_of(i * RB, RB)
            rows = pl.ds(row, RB)
            q = qz[rows, :]
            total = None
            for t in range(2):
                keys = kv_buf[half, pl.ds(4 * t, 4)].reshape(512, 128)
                s = dot_nt(q, keys)
                w = jnp.exp2(s * (0.125 * LOG2E))
                wexp[half, rows, pl.ds(512 * t, 512)] = w
                vals = kv1_buf[half, pl.ds(4 * t, 4)].reshape(512, 128)
                part = dot(w.astype(BF), vals)
                total = part if total is None else total + part
            if first:
                oacc[rows, :] = total
            else:
                oacc[rows, :] += total
            return carry

        lax.fori_loop(0, 1024 // RB, step, 0)

    def finish_forward():
        def step(b, carry):
            rows = pl.ds(pl.multiple_of(b * 128, 128), 128)
            o = oacc[rows, :]
            sw = swap(o)
            att = rnd(jnp.where(m128, 0.0, o / jnp.where(m128, 1.0, sw)))
            tot = jnp.where(m128, o, sw)
            inv_buf[rows, :] = 1.0 / tot
            att_send[b] = jnp.where(m64, swap(att[:64]), att[64:]).astype(BF)
            oacc[rows, :] = att
            return carry

        lax.fori_loop(0, 8, step, 0)

    def make_delta():
        def step(b, carry):
            rows = pl.ds(pl.multiple_of(b * 128, 128), 128)
            d = jnp.sum(oacc[rows, :] * gz[rows, :].astype(F32), axis=-1, keepdims=True)
            del_buf[rows, :] = jnp.broadcast_to(d, (128, 128))
            return carry

        lax.fori_loop(0, 8, step, 0)

    def backward(half, t, first):
        cols = pl.ds(512 * t, 512)
        dkvt[...] = jnp.zeros_like(dkvt)

        def step(i, carry):
            rows = pl.ds(pl.multiple_of(i * RB, RB), RB)
            qt = jnp.concatenate([qgt[2 * i], qgt[2 * i + 1]], axis=1)
            keys = kv_buf[half, pl.ds(4 * t, 4)].reshape(512, 128)
            dp = dot_nt(gz[rows, :], keys)
            p = wexp[half, rows, cols] * inv_buf[rows, 0:1]
            ds = (p * (dp - del_buf[rows, 0:1])).astype(BF)
            part = dot(ds, keys)
            dkvt[0:64, :] += dot(qt[0:64], ds)
            dkvt[64:128, :] += dot(qt[64:128], p.astype(BF))
            if first:
                dq_acc[rows, :] = part
            else:
                dq_acc[rows, :] += part
            return carry

        lax.fori_loop(0, 1024 // RB, step, 0)

    def key_grads(u):
        x = dkvt[:, u * 128 : u * 128 + 128].T
        return x * jnp.where(m128, 0.125, 1.0)

    def sdk_copy(p):
        return rcopy(dkv_x.at[p], dkv_sib.at[p], sdk_s.at[p], sdk_r.at[p], sibling)

    own_piece()
    @pl.when(diag)
    def _():
        pl.semaphore_wait(bar, 21)

    @pl.when(jnp.logical_not(diag))
    def _():
        pl.semaphore_wait(bar, 23)

    gather_far(K)
    gather_far(V)
    make_normed()
    loads[5].wait()
    loads[6].wait()
    for chunk in range(8):
        make_noise(chunk)
    gather_mid(K)
    gather_far(Q)
    make_uq()
    a2a_start(M_UQ, uq_send, uq_buf)
    gather_mid(V)
    gather_near(K)
    gather_far(O)
    make_ukv()
    gather_near(V)
    gather_sibling(K)
    gather_mid(Q)
    gather_last(K)
    form_weight(K)
    project_k()
    gather_near(Q)
    gather_sibling(V)
    gather_mid(O)
    gather_last(V)
    form_weight(V)
    project_v()
    a2a_start(M_KV, kv_send, kv_buf.at[0])
    gather_near(O)
    gather_sibling(Q)
    gather_last(Q)
    form_weight(Q)
    project_q()
    a2a_start(M_Q, q_send, q_buf)
    gather_sibling(O)
    forward_kv()
    gather_last(O)
    form_out()
    project_g()
    a2a_start(M_G, g_send, g_buf)
    ones_kv(0)
    a2a_wait_all(M_Q, q_send, q_buf)
    unpack_q()
    forward(0, True)
    for p in order:
        skv_copy(p).wait_recv()
    ones_kv(1)
    a2a_start(M_UKV, ukv_send, ukv_buf)
    forward(1, False)
    finish_forward()
    a2a_start(M_ATT, att_send, att_buf, True)
    a2a_wait_all(M_G, g_send, g_buf)
    unpack_g()
    make_delta()
    for t in range(2):
        backward(1, t, t == 0)
        for u in range(4):
            dkv_x[4 * t + u] = key_grads(u).astype(BF)
            start(sdk_copy(4 * t + u))
    a2a_wait_all(M_UKV, ukv_send, ukv_buf)
    a2a_wait_all(M_UQ, uq_send, uq_buf)
    scale_kv = None
    for t in range(2):
        backward(0, t, False)
        for p in range(4 * t, 4 * t + 4):
            sdk_copy(p).wait_recv()
            g = (key_grads(p - 4 * t) + dkv_sib[p].astype(F32)).astype(BF)
            dkv_send[p] = g
            g = g.astype(F32) * ukv_buf[p].astype(F32)
            scale_kv = g if scale_kv is None else scale_kv + g
        a2a_start(M_DKV, dkv_send, dkv_buf, True, range(4 * t, 4 * t + 4))
    scale_q = None
    for p in range(8):
        x = dq_acc[pl.ds(p * 128, 128), :] * 0.125
        g = jnp.where(m64, x[:64], swap(x[64:])).astype(BF)
        dq_send[p] = g
        g = g.astype(F32) * uq_buf[p].astype(F32)
        scale_q = g if scale_q is None else scale_q + g
    a2a_start(M_DQ, dq_send, dq_buf, True)
    scale_q = jnp.sum(scale_q, axis=0, keepdims=True)
    scale_q = scale_q + swap(scale_q)
    scale_kv = jnp.sum(scale_kv, axis=0, keepdims=True)
    idx_out[...] = idx_ref[...]
    first_row = lax.broadcasted_iota(jnp.int32, (8, 128), 0) == 0
    ps_buf[0, 0] = jnp.where(first_row, scale_q, scale_kv)

    def ps_copy(stage, k):
        to = (xgroup, ypeer, hpeer)[stage](k)
        return rcopy(ps_buf.at[stage, 0], ps_buf.at[stage, k], ps_s.at[stage, k], ps_r.at[stage, k], to)

    def ps_start(stage):
        for k in (4, 3, 5, 2, 6, 1, 7):
            start(ps_copy(stage, k))

    def ps_wait(stage):
        for k in (1, 7, 2, 6, 3, 5, 4):
            ps_copy(stage, k).wait_recv()

    def ps_sum(stage):
        ps_wait(stage)
        mine = (xl * 4 + xh * 2 + c, y)[stage]
        total = None
        for j in range(8):
            v = ps_buf[stage, (mine + 8 - j) % 8]
            total = v if total is None else total + v
        return total

    ps_start(0)

    def join_pair(a, b):
        a, b = a.astype(F32), b.astype(F32)
        return jnp.concatenate([jnp.where(m64, a, swap(b)), jnp.where(m64, swap(a), b)], 0)

    a2a_wait_all(M_ATT, att_send, att_buf, True)
    att_all = jnp.concatenate(
        [join_pair(att_buf[h], att_buf[h + 1]).astype(BF) for h in range(0, 8, 2)], axis=1
    )
    for t in range(2):
        att_out[:, pl.ds(512 * t, 512)] = dot(att_all, ow[:, pl.ds(512 * t, 512)]).astype(BF)
    ps_buf[1, 0] = ps_sum(0)
    ps_start(1)

    a2a_wait_all(M_DKV, dkv_send, dkv_buf, True)
    dks, dvs = [], []
    for h in range(0, 8, 2):
        a, b = dkv_buf[h].astype(F32), dkv_buf[h + 1].astype(F32)
        dks.append(jnp.where(m128, a, swap(b)))
        dvs.append(jnp.where(m128, swap(a), b))
    gkv = jnp.concatenate(dks + dvs, axis=1).astype(BF)
    grad = [dot_nt(gkv, wbuf[pl.ds(512 * t, 512), HD:]) for t in range(2)]
    ps_buf[2, 0] = ps_sum(1)
    ps_start(2)
    a2a_wait_all(M_DQ, dq_send, dq_buf, True)
    gq = [join_pair(dq_buf[h], dq_buf[h + 1]) for h in range(0, 8, 2)]
    gq = jnp.concatenate(gq, axis=1).astype(BF)
    grad = [grad[t] + dot_nt(gq, wbuf[pl.ds(512 * t, 512), :HD]) for t in range(2)]
    grad = jnp.concatenate(grad, axis=1)
    a = anch[...]
    r = lax.rsqrt(jnp.mean(a * a, axis=-1, keepdims=True) + 1e-06)
    d = grad * gain_ref[...]
    ga = r * (d - a * (r * r * jnp.mean(d * a, axis=-1, keepdims=True)))
    hi = ga.astype(BF)
    hi_out[...] = hi
    lo_out[...] = (ga - hi.astype(F32)).astype(BF)
    ps_wait(2)
    m8 = left_half(8)
    for j in range(4):
        a, b = (ps_buf[2, (z + 8 - h) % 8] for h in (2 * j, 2 * j + 1))
        qk = jnp.where(m8, a, swap(b))
        gs_out[j : j + 1, :] = qk[0:1]
        gs_out[4 + j : 5 + j, :] = qk[1:2]
        gs_out[8 + j : 9 + j, :] = jnp.where(m8, swap(a), b)[1:2]

    for copy in sends:
        copy.wait_send()

    @pl.when(jnp.logical_not(diag))
    def _():
        for msg, src, dst, back in (
            (M_KV, kv_send, kv_buf.at[0], False),
            (M_Q, q_send, q_buf, False),
            (M_G, g_send, g_buf, False),
            (M_UKV, ukv_send, ukv_buf, False),
            (M_UQ, uq_send, uq_buf, False),
            (M_ATT, att_send, att_buf, True),
            (M_DQ, dq_send, dq_buf, True),
            (M_DKV, dkv_send, dkv_buf, True),
        ):
            a2a_one(msg, src, dst, 3, back).wait_send()


def finish(idx_ref, att_ref, hi_ref, lo_ref, gs_ref, att_out, gp_out, gs_out):
    sel_t = (lax.broadcasted_iota(jnp.int32, (PTS, TOK), 0) == idx_ref[...]).astype(BF)
    sel2 = jnp.concatenate([sel_t, sel_t], axis=1)
    for t in range(2):
        cols = pl.ds(512 * t, 512)
        gp_out[:, cols] = dot(sel2, jnp.concatenate([hi_ref[:, cols], lo_ref[:, cols]], axis=0))
    att_out[...] = att_ref[...]
    gs_out[...] = gs_ref[...]


def local(points, anchor_index, norm_gain, weight_mean, weight_scale, noise_seed, out_weight, cotangent):
    vm = pl.BlockSpec(memory_space=pltpu.VMEM)
    hbm = pl.BlockSpec(memory_space=pltpu.HBM)
    V_ = pltpu.VMEM
    dma = pltpu.SemaphoreType.DMA
    att, hi, lo, gs, idx = pl.pallas_call(
        body,
        out_shape=(
            jax.ShapeDtypeStruct((TOK, D), BF),
            jax.ShapeDtypeStruct((TOK, D), BF),
            jax.ShapeDtypeStruct((TOK, D), BF),
            jax.ShapeDtypeStruct((12, 128), F32),
            jax.ShapeDtypeStruct((1, TOK), jnp.int32),
        ),
        in_specs=[hbm] * 8,
        out_specs=(vm, vm, vm, vm, vm),
        scratch_shapes=[
            V_((PTS, D), BF),
            V_((TOK, D), BF),
            V_((1, TOK), jnp.int32),
            V_((1, D), F32),
            V_((32, 3 * HD), BF),
            V_((12, 128), F32),
            V_((12, 128), jnp.int32),
            V_((16, D), BF),
            V_((3, 4, 2, 2, 8, 32, 128), BF),
            V_((4, 2, 2, 8, 16, 256), BF),
            V_((HD, D), BF),
            V_((D, 3 * HD), F32),
            V_((D, 3 * HD), BF),
            V_((D, 3 * HD), BF),
            V_((TOK, D), F32),
            V_((TOK, D), BF),
            V_((TOK, HD), F32),
            V_((8, 128, 128), BF),
            V_((8, 64, 128), BF),
            V_((8, 64, 128), BF),
            V_((8, 128, 128), BF),
            V_((8, 64, 128), BF),
            V_((2, 8, 128, 128), BF),
            V_((2, 8, 128, 128), BF),
            V_((8, 64, 128), BF),
            V_((8, 64, 128), BF),
            V_((8, 128, 128), BF),
            V_((8, 64, 128), BF),
            V_((1024, 128), BF),
            V_((1024, 128), BF),
            V_((8, 128, 128), BF),
            V_((2, 1024, 1024), F32),
            V_((1024, 128), F32),
            V_((1024, 128), F32),
            V_((1024, 128), F32),
            V_((1024, 128), F32),
            V_((128, 512), F32),
            V_((8, 128, 128), BF),
            V_((8, 128, 128), BF),
            V_((8, 128, 128), BF),
            V_((8, 64, 128), BF),
            V_((8, 64, 128), BF),
            V_((8, 64, 128), BF),
            V_((8, 64, 128), BF),
            V_((8, 128, 128), BF),
            V_((3, 8, 8, 128), F32),
            dma((8,)),
            dma((4, 8)),
            dma((4, 8)),
            dma((4,)),
            dma((4,)),
            dma((4, 2, 3)),
            dma((4, 2, 3)),
            dma((4, 5)),
            dma((4, 5)),
            dma((8, 8)),
            dma((8, 8)),
            dma((8,)),
            dma((8,)),
            dma((8,)),
            dma((8,)),
            dma((3, 8)),
            dma((3, 8)),
        ],
        compiler_params=pltpu.CompilerParams(
            collective_id=0, has_side_effects=True, vmem_limit_bytes=44 * 1024 * 1024
        ),
    )(*(
        pltpu.with_memory_space_constraint(x, pltpu.HBM)
        for x in (
            points[0],
            anchor_index,
            norm_gain.reshape(1, D),
            weight_mean,
            weight_scale.reshape(12, 128),
            noise_seed.reshape(12, 128),
            out_weight,
            cotangent[0],
        )
    ))
    att, gpts, gs = pl.pallas_call(
        finish,
        out_shape=(
            jax.ShapeDtypeStruct((TOK, D), BF),
            jax.ShapeDtypeStruct((PTS, D), F32),
            jax.ShapeDtypeStruct((12, 128), F32),
        ),
        in_specs=[vm] * 5,
        out_specs=(vm, vm, vm),
        compiler_params=pltpu.CompilerParams(vmem_limit_bytes=8 * 1024 * 1024),
    )(idx, att, hi, lo, gs)
    return att[None], gpts[None], gs.reshape(3 * HD)


def solution(mesh):
    in_specs = (
        P("outer", "inner", None),
        P("outer", "inner"),
        P(),
        P("outer", None),
        P(),
        P(),
        P("outer", None),
        P("outer", "inner", None),
    )
    out_specs = (P("outer", "inner", None), P("outer", "inner", None), P())
    return jax.shard_map(local, mesh=mesh, in_specs=in_specs, out_specs=out_specs, check_vma=False)
```

time: 113 us -> 84.2 us (0.75)
  Pallas kernels: 105 us -> 83.4 us
  local copies, waits for them, and re-layouts: 6.56 us -> 0 us
    pallas_call x1, Pallas kernels: 105 us -> 82.1 us  [local(): pl.pallas_call(body, out_shape=(jax.ShapeDtypeStruct((TOK, D), BF), jax.S...]
    unnamed x6 -> x0, local copies, waits for them, and re-layouts: 4.66 us -> none
    reshape x2 -> x0, local copies, waits for them, and re-layouts: 1.9 us -> none  [the longest x1 1.3 us: local(): weight_scale.reshape(1, 3 * HD)]
    pallas_call x0 -> x1, Pallas kernels: none -> 1.3 us  [local(): pl.pallas_call(finish, out_shape=(jax.ShapeDtypeStruct((TOK, D), BF), jax...]
where the time goes in v2:
time: 84.2 us; the launch traced here: 84 us
  Pallas kernels  83.4 us (99%)
    pallas_call x1, Pallas kernels, local(): pl.pallas_call(body, out_shape=(jax.ShapeDtypeStruct((TOK, D), BF), jax.S...  82.1 us

profile of v2, /device:TPU:1, one launch (start us, length us, event | category | flops | bytes accessed | tf_op | source)
XLA Modules:
  0.0 84.0 jit_solution(7438189604624561560)
XLA Ops:
  0.6 82.1 %shard_map.103 = (bf16[128,1024]{1,0:T(8,128)(2,1)S(1)}, bf16[128,1024]{1,0:T(8,128)(2,1)S(1)}, bf16[128,1024]{1,0:T(8,128)(2,1)S(1)}, f32[12,128]{1,0:T(8,128)S(1)}, s32[1,128]{1,0:T(1,128)S(1)}) custom-call(bf16[256,1024]{1,0:T(8,128)(2,1)} %bitcast.8, s32[1,128]{1,0:T(1,128)} %idx_hbm.1, f32[1,1024]{1,0:T(1,128)} %bitcast.12, bf16[32,1536]{1,0:T(8,128)(2,1)} %mean_hbm.1, ...), custom_call_target="tpu_custom_call" | custom-call | tf_op jit(solution)/shard_map/pallas_call | solution.py:724
  82.7 1.3 %shard_map.104 = (bf16[128,1024]{1,0:T(8,128)(2,1)}, f32[256,1024]{1,0:T(8,128)}, f32[12,128]{1,0:T(8,128)}) custom-call(s32[1,128]{1,0:T(1,128)S(1)} %get-tuple-element.11.idx_ref, bf16[128,1024]{1,0:T(8,128)(2,1)S(1)} %get-tuple-element.12.att_ref, bf16[128,1024]{1,0:T(8,128)(2,1)S(1)} %get-tuple-element.13.hi_ref, ...), custom_call_target="tpu_custom_call" | custom-call | tf_op jit(solution)/shard_map/pallas_call | solution.py:816

commit v3 on v2

--- a/solution.py
+++ b/solution.py
@@ -134,6 +134,9 @@
         g = (xl * 4 + xh * 2 + c + k) % 8
         return dev(z, g // 4, y, (g // 2) % 2, g % 2)
 
+    def cross(k):
+        return dev(z, 1 - xl, (y + k) % NY, 1 - xh, c)
+
     def zpeer(k):
         return dev((z + k) % NZ, xl, y, xh, c)
 
@@ -425,17 +428,13 @@
             kv1_buf[half, b] = jnp.where(m128, 1.0, kv_buf[half, b].astype(F32)).astype(BF)
             return carry
 
-        lax.fori_loop(0, 8, step, 0)
-
-    def unpack_q():
-        def step(b, carry):
-            p = q_buf[b].astype(F32)
-            zero = jnp.zeros_like(p)
-            full = jnp.concatenate([jnp.where(m64, p, zero), jnp.where(m64, swap(p), zero)], 0)
-            qz[pl.ds(pl.multiple_of(b * 128, 128), 128), :] = full.astype(BF)
-            return carry
-
-        lax.fori_loop(0, 8, step, 0)
+        lax.fori_loop(0, 8, step, 0, unroll=True)
+
+    def unpack_q(b):
+        p = q_buf[b].astype(F32)
+        zero = jnp.zeros_like(p)
+        full = jnp.concatenate([jnp.where(m64, p, zero), jnp.where(m64, swap(p), zero)], 0)
+        qz[pl.ds(b * 128, 128), :] = full.astype(BF)
 
     def unpack_g():
         def step(b, carry):
@@ -448,28 +447,42 @@
             qgt[b] = both.T.astype(BF)
             return carry
 
-        lax.fori_loop(0, 8, step, 0)
-
-    RB = 256
-
-    def forward(half, first):
+        lax.fori_loop(0, 8, step, 0, unroll=True)
+
+    RB = 512
+
+    def forward_rows(half, i, first):
+        rows = pl.ds(pl.multiple_of(i * RB, RB), RB)
+        q = qz[rows, :]
+        total = None
+        for t in range(2):
+            keys = kv_buf[half, pl.ds(4 * t, 4)].reshape(512, 128)
+            s = dot_nt(q, keys)
+            w = jnp.exp2(s * (0.125 * LOG2E))
+            wexp[half, rows, pl.ds(512 * t, 512)] = w
+            vals = kv1_buf[half, pl.ds(4 * t, 4)].reshape(512, 128)
+            part = dot(w.astype(BF), vals)
+            total = part if total is None else total + part
+        if first:
+            oacc[rows, :] = total
+        else:
+            oacc[rows, :] += total
+
+    def forward_first():
+        for p in order:
+            a2a_wait(M_Q, q_send, q_buf, p)
+        for p in range(8):
+            unpack_q(p)
+
         def step(i, carry):
-            row = pl.multiple_of(i * RB, RB)
-            rows = pl.ds(row, RB)
-            q = qz[rows, :]
-            total = None
-            for t in range(2):
-                keys = kv_buf[half, pl.ds(4 * t, 4)].reshape(512, 128)
-                s = dot_nt(q, keys)
-                w = jnp.exp2(s * (0.125 * LOG2E))
-                wexp[half, rows, pl.ds(512 * t, 512)] = w
-                vals = kv1_buf[half, pl.ds(4 * t, 4)].reshape(512, 128)
-                part = dot(w.astype(BF), vals)
-                total = part if total is None else total + part
-            if first:
-                oacc[rows, :] = total
-            else:
-                oacc[rows, :] += total
+            forward_rows(0, i, True)
+            return carry
+
+        lax.fori_loop(0, 1024 // RB, step, 0)
+
+    def forward_second():
+        def step(i, carry):
+            forward_rows(1, i, False)
             return carry
 
         lax.fori_loop(0, 1024 // RB, step, 0)
@@ -486,7 +499,7 @@
             oacc[rows, :] = att
             return carry
 
-        lax.fori_loop(0, 8, step, 0)
+        lax.fori_loop(0, 8, step, 0, unroll=True)
 
     def make_delta():
         def step(b, carry):
@@ -495,15 +508,16 @@
             del_buf[rows, :] = jnp.broadcast_to(d, (128, 128))
             return carry
 
-        lax.fori_loop(0, 8, step, 0)
-
-    def backward(half, t, first):
+        lax.fori_loop(0, 8, step, 0, unroll=True)
+
+    def backward(half, t, first, start_row=0, stop_row=1024):
         cols = pl.ds(512 * t, 512)
-        dkvt[...] = jnp.zeros_like(dkvt)
+        if start_row == 0:
+            dkvt[...] = jnp.zeros_like(dkvt)
 
         def step(i, carry):
             rows = pl.ds(pl.multiple_of(i * RB, RB), RB)
-            qt = jnp.concatenate([qgt[2 * i], qgt[2 * i + 1]], axis=1)
+            qt = jnp.concatenate([qgt[RB // 128 * i + n] for n in range(RB // 128)], axis=1)
             keys = kv_buf[half, pl.ds(4 * t, 4)].reshape(512, 128)
             dp = dot_nt(gz[rows, :], keys)
             p = wexp[half, rows, cols] * inv_buf[rows, 0:1]
@@ -517,7 +531,7 @@
                 dq_acc[rows, :] += part
             return carry
 
-        lax.fori_loop(0, 1024 // RB, step, 0)
+        lax.fori_loop(start_row // RB, stop_row // RB, step, 0)
 
     def key_grads(u):
         x = dkvt[:, u * 128 : u * 128 + 128].T
@@ -545,7 +559,6 @@
     gather_mid(K)
     gather_far(Q)
     make_uq()
-    a2a_start(M_UQ, uq_send, uq_buf)
     gather_mid(V)
     gather_near(K)
     gather_far(O)
@@ -575,15 +588,14 @@
     form_out()
     project_g()
     a2a_start(M_G, g_send, g_buf)
+    a2a_start(M_UKV, ukv_send, ukv_buf)
+    a2a_start(M_UQ, uq_send, uq_buf)
     ones_kv(0)
-    a2a_wait_all(M_Q, q_send, q_buf)
-    unpack_q()
-    forward(0, True)
+    forward_first()
     for p in order:
         skv_copy(p).wait_recv()
     ones_kv(1)
-    a2a_start(M_UKV, ukv_send, ukv_buf)
-    forward(1, False)
+    forward_second()
     finish_forward()
     a2a_start(M_ATT, att_send, att_buf, True)
     a2a_wait_all(M_G, g_send, g_buf)
@@ -594,26 +606,32 @@
         for u in range(4):
             dkv_x[4 * t + u] = key_grads(u).astype(BF)
             start(sdk_copy(4 * t + u))
+    def send_dq(slots):
+        for p in slots:
+            x = dq_acc[pl.ds(p * 128, 128), :] * 0.125
+            dq_send[p] = jnp.where(m64, x[:64], swap(x[64:])).astype(BF)
+        a2a_start(M_DQ, dq_send, dq_buf, True, slots)
+
+    def send_dkv(slots):
+        for u, p in enumerate(slots):
+            sdk_copy(p).wait_recv()
+            dkv_send[p] = (key_grads(u) + dkv_sib[p].astype(F32)).astype(BF)
+        a2a_start(M_DKV, dkv_send, dkv_buf, True, slots)
+
+    backward(0, 0, False)
+    send_dkv(range(4))
+    backward(0, 1, False, 0, 512)
+    send_dq(range(4))
+    backward(0, 1, False, 512, 1024)
+    send_dkv(range(4, 8))
+    send_dq(range(4, 8))
     a2a_wait_all(M_UKV, ukv_send, ukv_buf)
     a2a_wait_all(M_UQ, uq_send, uq_buf)
-    scale_kv = None
-    for t in range(2):
-        backward(0, t, False)
-        for p in range(4 * t, 4 * t + 4):
-            sdk_copy(p).wait_recv()
-            g = (key_grads(p - 4 * t) + dkv_sib[p].astype(F32)).astype(BF)
-            dkv_send[p] = g
-            g = g.astype(F32) * ukv_buf[p].astype(F32)
-            scale_kv = g if scale_kv is None else scale_kv + g
-        a2a_start(M_DKV, dkv_send, dkv_buf, True, range(4 * t, 4 * t + 4))
-    scale_q = None
-    for p in range(8):
-        x = dq_acc[pl.ds(p * 128, 128), :] * 0.125
-        g = jnp.where(m64, x[:64], swap(x[64:])).astype(BF)
-        dq_send[p] = g
-        g = g.astype(F32) * uq_buf[p].astype(F32)
-        scale_q = g if scale_q is None else scale_q + g
-    a2a_start(M_DQ, dq_send, dq_buf, True)
+    scale_kv = dkv_send[0].astype(F32) * ukv_buf[0].astype(F32)
+    scale_q = dq_send[0].astype(F32) * uq_buf[0].astype(F32)
+    for p in range(1, 8):
+        scale_kv = scale_kv + dkv_send[p].astype(F32) * ukv_buf[p].astype(F32)
+        scale_q = scale_q + dq_send[p].astype(F32) * uq_buf[p].astype(F32)
     scale_q = jnp.sum(scale_q, axis=0, keepdims=True)
     scale_q = scale_q + swap(scale_q)
     scale_kv = jnp.sum(scale_kv, axis=0, keepdims=True)
@@ -664,9 +682,10 @@
         dks.append(jnp.where(m128, a, swap(b)))
         dvs.append(jnp.where(m128, swap(a), b))
     gkv = jnp.concatenate(dks + dvs, axis=1).astype(BF)
-    grad = [dot_nt(gkv, wbuf[pl.ds(512 * t, 512), HD:]) for t in range(2)]
+    grad = [dot_nt(gkv, wbuf[pl.ds(0, 512), HD:])]
     ps_buf[2, 0] = ps_sum(1)
     ps_start(2)
+    grad.append(dot_nt(gkv, wbuf[pl.ds(512, 512), HD:]))
     a2a_wait_all(M_DQ, dq_send, dq_buf, True)
     gq = [join_pair(dq_buf[h], dq_buf[h + 1]) for h in range(0, 8, 2)]
     gq = jnp.concatenate(gq, axis=1).astype(BF)

time: 84.2 us -> 81.5 us (0.968)
  Pallas kernels: 83.4 us -> 80.7 us
    pallas_call x1, Pallas kernels: 82.1 us -> 79.4 us  [local(): pl.pallas_call(body, out_shape=(jax.ShapeDtypeStruct((TOK, D), BF), jax.S...]
where the time goes in v3:
time: 81.5 us; the launch traced here: 81.3 us
  Pallas kernels  80.7 us (99%)
    pallas_call x1, Pallas kernels, local(): pl.pallas_call(body, out_shape=(jax.ShapeDtypeStruct((TOK, D), BF), jax.S...  79.4 us

profile of v3, /device:TPU:1, one launch (start us, length us, event | category | flops | bytes accessed | tf_op | source)
XLA Modules:
  0.0 81.3 jit_solution(12136139279123203965)
XLA Ops:
  0.6 79.4 %shard_map.103 = (bf16[128,1024]{1,0:T(8,128)(2,1)S(1)}, bf16[128,1024]{1,0:T(8,128)(2,1)S(1)}, bf16[128,1024]{1,0:T(8,128)(2,1)S(1)}, f32[12,128]{1,0:T(8,128)S(1)}, s32[1,128]{1,0:T(1,128)S(1)}) custom-call(bf16[256,1024]{1,0:T(8,128)(2,1)} %bitcast.8, s32[1,128]{1,0:T(1,128)} %idx_hbm.1, f32[1,1024]{1,0:T(1,128)} %bitcast.12, bf16[32,1536]{1,0:T(8,128)(2,1)} %mean_hbm.1, ...), custom_call_target="tpu_custom_call" | custom-call | tf_op jit(solution)/shard_map/pallas_call | solution.py:743
  80.0 1.3 %shard_map.104 = (bf16[128,1024]{1,0:T(8,128)(2,1)}, f32[256,1024]{1,0:T(8,128)}, f32[12,128]{1,0:T(8,128)}) custom-call(s32[1,128]{1,0:T(1,128)S(1)} %get-tuple-element.11.idx_ref, bf16[128,1024]{1,0:T(8,128)(2,1)S(1)} %get-tuple-element.12.att_ref, bf16[128,1024]{1,0:T(8,128)(2,1)S(1)} %get-tuple-element.13.hi_ref, ...), custom_call_target="tpu_custom_call" | custom-call | tf_op jit(solution)/shard_map/pallas_call | solution.py:835

commit v4 on v3

--- a/solution.py
+++ b/solution.py
@@ -618,6 +618,7 @@
             dkv_send[p] = (key_grads(u) + dkv_sib[p].astype(F32)).astype(BF)
         a2a_start(M_DKV, dkv_send, dkv_buf, True, slots)
 
+    early = len(sends)
     backward(0, 0, False)
     send_dkv(range(4))
     backward(0, 1, False, 0, 512)
@@ -661,6 +662,10 @@
         return total
 
     ps_start(0)
+
+    for copy in sends[:early]:
+        copy.wait_send()
+    last_sends = sends[early:]
 
     def join_pair(a, b):
         a, b = a.astype(F32), b.astype(F32)
@@ -707,7 +712,7 @@
         gs_out[4 + j : 5 + j, :] = qk[1:2]
         gs_out[8 + j : 9 + j, :] = jnp.where(m8, swap(a), b)[1:2]
 
-    for copy in sends:
+    for copy in last_sends + sends[early + len(last_sends) :]:
         copy.wait_send()
 
     @pl.when(jnp.logical_not(diag))

time: 81.5 us -> 81.3 us (level)
  no operation moved by 1% of the time
where the time goes in v4:
time: 81.3 us; the launch traced here: 81.1 us
  Pallas kernels  80.5 us (99%)
    pallas_call x1, Pallas kernels, local(): pl.pallas_call(body, out_shape=(jax.ShapeDtypeStruct((TOK, D), BF), jax.S...  79.2 us

profile of v4, /device:TPU:1, one launch (start us, length us, event | category | flops | bytes accessed | tf_op | source)
XLA Modules:
  0.0 81.1 jit_solution(17061838919814872194)
XLA Ops:
  0.6 79.2 %shard_map.103 = (bf16[128,1024]{1,0:T(8,128)(2,1)S(1)}, bf16[128,1024]{1,0:T(8,128)(2,1)S(1)}, bf16[128,1024]{1,0:T(8,128)(2,1)S(1)}, f32[12,128]{1,0:T(8,128)S(1)}, s32[1,128]{1,0:T(1,128)S(1)}) custom-call(bf16[256,1024]{1,0:T(8,128)(2,1)} %bitcast.8, s32[1,128]{1,0:T(1,128)} %idx_hbm.1, f32[1,1024]{1,0:T(1,128)} %bitcast.12, bf16[32,1536]{1,0:T(8,128)(2,1)} %mean_hbm.1, ...), custom_call_target="tpu_custom_call" | custom-call | tf_op jit(solution)/shard_map/pallas_call | solution.py:748
  79.8 1.3 %shard_map.104 = (bf16[128,1024]{1,0:T(8,128)(2,1)}, f32[256,1024]{1,0:T(8,128)}, f32[12,128]{1,0:T(8,128)}) custom-call(s32[1,128]{1,0:T(1,128)S(1)} %get-tuple-element.11.idx_ref, bf16[128,1024]{1,0:T(8,128)(2,1)S(1)} %get-tuple-element.12.att_ref, bf16[128,1024]{1,0:T(8,128)(2,1)S(1)} %get-tuple-element.13.hi_ref, ...), custom_call_target="tpu_custom_call" | custom-call | tf_op jit(solution)/shard_map/pallas_call | solution.py:840
